TPU v7x, 32 devices: a whole 2x2x4 slice. The times are simulated.
32 devices in a mesh: seq: 8 (over z, x), dp: 4 (over y, core).
Axes of the slice: x: 2, y: 2, z: 4, core: 2. Of those that a mesh axis runs over, the one named last changes fastest.
Arguments:
- query: bfloat16 [4, 4096, 2048], P('dp', 'seq'), may hold values from -100 to 100
- key: bfloat16 [4, 4096, 2048], P('dp', 'seq'), may hold values from -6 to 6
- value: bfloat16 [4, 4096, 2048], P('dp', 'seq'), may hold values from -6 to 6
- grad_ctx: bfloat16 [4, 4096, 2048], P('dp', 'seq'), may hold values from -6 to 6
- proj_key: bfloat16 [512, 4096], P(None, 'seq'), may hold values from -0.09375 to 0.09375
- proj_value: bfloat16 [512, 4096], P(None, 'seq'), may hold values from -0.09375 to 0.09375
Outputs:
- grad_query: bfloat16 [4, 4096, 2048], P('dp', 'seq')
- grad_key: bfloat16 [4, 4096, 2048], P('dp', 'seq')
- grad_value: bfloat16 [4, 4096, 2048], P('dp', 'seq')
- grad_proj_key: bfloat16 [512, 4096], P('dp', 'seq')
- grad_proj_value: bfloat16 [512, 4096], P('dp', 'seq')
All inputs are finite; a program needn't handle non-finite values.
Results may differ from a plain program's by a relative error of at most 0.034.
The roundings to bfloat16 on the way count: a program that leaves them out, or rounds other values in their place, can miss the bound.
Values may be sent and summed in bfloat16 or wider, within the bound.
A program may use at most 128 MiB of HBM per device.

v0:
```python
import functools

import jax
import jax.numpy as jnp
from jax import lax
from jax.experimental import pallas as pl
from jax.experimental.pallas import tpu as pltpu
from jax.sharding import PartitionSpec as P

HEAD_DIM = 128
INNER = 2
RECV = 8
SLOTS = 8
A, B, C, D, E, F, G, Z, I = 0, 2, 4, 6, 8, 10, 12, 14, 16
NT = (((1,), (1,)), ((), ()))


def dot(a, b):
    return jnp.dot(a, b, preferred_element_type=jnp.float32)


def dot_nt(a, b):
    return lax.dot_general(a, b, NT, preferred_element_type=jnp.float32)


def kernel(
    n_seq, n_dp,
    q_ref, k_ref, v_ref, g_ref, pk_ref, pv_ref,
    gq_ref, gk_ref, gv_ref, sk_ref, sv_ref,
    own_k, own_v, snd_k, snd_v, half_v, arr_k, arr_v, blk_k, blk_v, full,
    own_d, snd_d, half_d, arr_d, blk_d, full_d,
    term, snd_t, arr_t, pkt_ref, pvt_ref,
    s_pair, r_pair, s_grp, r_grp, s_dp, r_dp,
):
    kp_rows = pk_ref.shape[0]
    n_chunks = q_ref.shape[1] // HEAD_DIM
    n_out = n_seq // INNER
    half = kp_rows // INNER
    blk = half // n_out
    t_rows = kp_rows // n_dp
    scale = HEAD_DIM ** (-0.5)
    bf = jnp.bfloat16

    seq = lax.axis_index("seq")
    dp = lax.axis_index("dp")
    x = lax.rem(seq, INNER)
    z = seq // INNER
    mate = seq + 1 - 2 * x
    mine = pl.multiple_of(x * half, half)
    other = pl.multiple_of((1 - x) * half, half)

    def z_at(j):
        return lax.rem(z + j, n_out)

    def peer(j):
        return z_at(j) * INNER + x

    barrier = pltpu.get_barrier_semaphore()
    pl.semaphore_signal(barrier, inc=1, device_id={"seq": mate})
    for j in range(1, n_out):
        pl.semaphore_signal(barrier, inc=1, device_id={"seq": peer(j)})
    for j in range(1, n_dp):
        pl.semaphore_signal(barrier, inc=1, device_id={"dp": lax.rem(dp + j, n_dp)})
    pl.semaphore_wait(barrier, 1 + (n_out - 1) + (n_dp - 1))

    def cols(c):
        return pl.ds(pl.multiple_of(c * HEAD_DIM, HEAD_DIM), HEAD_DIM)

    def pair_copy(kind, src, dst, c):
        return pltpu.make_async_remote_copy(
            src_ref=src, dst_ref=dst,
            send_sem=s_pair.at[kind, lax.rem(c, SLOTS)],
            recv_sem=r_pair.at[kind, lax.rem(c, RECV)],
            device_id={"seq": mate},
        )

    def grp_copy(kind, j, src, dst, c):
        return pltpu.make_async_remote_copy(
            src_ref=src, dst_ref=dst,
            send_sem=s_grp.at[kind, j - 1, lax.rem(c, SLOTS)],
            recv_sem=r_grp.at[kind, j - 1, lax.rem(c, RECV)],
            device_id={"seq": peer(j)},
        )

    def a_copies(c):
        s = lax.rem(c, SLOTS)
        return [
            pair_copy(0, snd_k.at[s], arr_k.at[c], c),
            pair_copy(1, snd_v.at[s], arr_v.at[c], c),
        ]

    def b_copies(c):
        s = lax.rem(c, SLOTS)
        out = []
        for j in range(1, n_out):
            rows = pl.ds(pl.multiple_of(z_at(j) * blk, blk), blk)
            out.append(grp_copy(0, j, own_k.at[s, rows], blk_k.at[c, j - 1], c))
            out.append(grp_copy(1, j, half_v.at[s, rows], blk_v.at[c, j - 1], c))
        return out

    own_rows = pl.ds(pl.multiple_of(x * half + z * blk, blk), blk)
    half_rows = pl.ds(mine, half)
    in_half = pl.ds(pl.multiple_of(z * blk, blk), blk)

    def gather_copies(kind, buf, c):
        ref = buf.at[c, :, own_rows]
        return [grp_copy(kind, j, ref, ref, c) for j in range(1, n_out)]

    def mate_copies(kind, buf, c):
        ref = buf.at[c, :, half_rows]
        return [pair_copy(kind, ref, ref, c)]

    def e_copies(c):
        return [pair_copy(3, snd_d.at[lax.rem(c, SLOTS)], arr_d.at[c], c)]

    def f_copies(c):
        s = lax.rem(c, SLOTS)
        out = []
        for j in range(1, n_out):
            rows = pl.ds(pl.multiple_of(z_at(j) * blk, blk), blk)
            out.append(grp_copy(3, j, half_d.at[s, :, rows], blk_d.at[c, j - 1], c))
        return out

    def start(copies):
        for copy in copies:
            copy.start()

    def wait(copies):
        for copy in copies:
            copy.wait()

    def stage_a(c):
        s = lax.rem(c, SLOTS)
        kc = k_ref[:, cols(c)]
        vc = v_ref[:, cols(c)]
        snd_k[s] = dot(pk_ref[pl.ds(other, half), :], kc)
        snd_v[s] = dot(pv_ref[pl.ds(other, half), :], vc).astype(bf)
        start(a_copies(c))
        own_k[s] = dot(pk_ref[pl.ds(mine, half), :], kc)
        own_v[s] = dot(pv_ref[pl.ds(mine, half), :], vc)

    def stage_b(c):
        s = lax.rem(c, SLOTS)
        wait(a_copies(c))
        own_k[s] = own_k[s] + arr_k[c]
        both = own_v[s] + arr_v[c].astype(jnp.float32)
        own_v[s] = both
        half_v[s] = both.astype(bf)
        start(b_copies(c))

    def stage_c(c):
        s = lax.rem(c, SLOTS)
        wait(b_copies(c))
        kt = own_k[s, in_half]
        vt = own_v[s, in_half]
        for j in range(1, n_out):
            kt += blk_k[c, j - 1]
            vt += blk_v[c, j - 1].astype(jnp.float32)
        full[c, 0, own_rows] = kt.astype(bf)
        full[c, 1, own_rows] = vt.astype(bf)
        start(gather_copies(2, full, c))

    def stage_d(c):
        wait(gather_copies(2, full, c))
        start(mate_copies(2, full, c))

    def stage_e(c):
        s = lax.rem(c, SLOTS)
        wait(mate_copies(2, full, c))
        kp = full[c, 0]
        vp = full[c, 1]
        kpt = kp.astype(jnp.float32).T.astype(bf)
        n_pos = q_ref.shape[0]
        step = min(256, n_pos)
        dk = jnp.zeros((kp_rows, HEAD_DIM), jnp.float32)
        dv = jnp.zeros((kp_rows, HEAD_DIM), jnp.float32)
        for p in range(0, n_pos, step):
            qb = q_ref[pl.ds(p, step), cols(c)]
            gb = g_ref[pl.ds(p, step), cols(c)]
            scores = dot_nt(kp, qb) * scale
            e = jnp.exp(scores - jnp.max(scores, axis=0, keepdims=True))
            probs = e * (1.0 / jnp.sum(e, axis=0, keepdims=True))
            dv += dot(probs.astype(bf), gb)
            gp = dot_nt(vp, gb)
            delta = jnp.sum(probs * gp, axis=0, keepdims=True)
            gs = (probs * (gp - delta) * scale).astype(bf)
            dk += dot(gs, qb)
            gq_ref[pl.ds(p, step), cols(c)] = dot(kpt, gs).T.astype(bf)
        own_d[s, 0] = jnp.where(x == 0, dk[:half], dk[half:])
        own_d[s, 1] = jnp.where(x == 0, dv[:half], dv[half:])
        snd_d[s, 0] = jnp.where(x == 0, dk[half:], dk[:half]).astype(bf)
        snd_d[s, 1] = jnp.where(x == 0, dv[half:], dv[:half]).astype(bf)
        start(e_copies(c))

    def stage_f(c):
        s = lax.rem(c, SLOTS)
        wait(e_copies(c))
        both = own_d[s] + arr_d[c].astype(jnp.float32)
        own_d[s] = both
        half_d[s] = both.astype(bf)
        start(f_copies(c))

    def stage_g(c):
        s = lax.rem(c, SLOTS)
        wait(f_copies(c))
        total = own_d[s, :, in_half]
        for j in range(1, n_out):
            total += blk_d[c, j - 1].astype(jnp.float32)
        full_d[c, :, own_rows] = total.astype(bf)
        start(gather_copies(4, full_d, c))

    def stage_z(c):
        wait(gather_copies(4, full_d, c))
        start(mate_copies(4, full_d, c))

    def stage_i(c):
        wait(mate_copies(4, full_d, c))
        dkp = full_d[c, 0]
        dvp = full_d[c, 1]
        gk_ref[:, cols(c)] = dot(pkt_ref[...], dkp).astype(bf)
        gv_ref[:, cols(c)] = dot(pvt_ref[...], dvp).astype(bf)
        term[0] += dot_nt(dkp, k_ref[:, cols(c)])
        term[1] += dot_nt(dvp, v_ref[:, cols(c)])

    term[...] = jnp.zeros_like(term)

    stages = (
        (A, stage_a), (Z, stage_z), (D, stage_d), (G, stage_g), (F, stage_f), (C, stage_c),
        (B, stage_b), (E, stage_e), (I, stage_i),
    )

    def turn():
        pkt_ref[...] = pk_ref[...].astype(jnp.float32).T.astype(bf)
        pvt_ref[...] = pv_ref[...].astype(jnp.float32).T.astype(bf)

    def iteration(i, _):
        pl.when(i == 1)(turn)
        for at, stage in stages:
            pl.when((i >= at) & (i < at + n_chunks))(functools.partial(stage, i - at))
        return 0

    lax.fori_loop(0, n_chunks + I, iteration, 0)

    snd_t[...] = term[...].astype(bf)
    copies = []
    for j in range(1, n_dp):
        to = lax.rem(dp + j, n_dp)
        rows = pl.ds(pl.multiple_of(to * t_rows, t_rows), t_rows)
        copies.append(
            pltpu.make_async_remote_copy(
                src_ref=snd_t.at[:, rows], dst_ref=arr_t.at[j - 1],
                send_sem=s_dp.at[j - 1], recv_sem=r_dp.at[j - 1],
                device_id={"dp": to},
            )
        )
    start(copies)
    wait(copies)
    total = term[:, pl.ds(pl.multiple_of(dp * t_rows, t_rows), t_rows)]
    for j in range(1, n_dp):
        total += arr_t[j - 1].astype(jnp.float32)
    sk_ref[...] = total[0].astype(bf)
    sv_ref[...] = total[1].astype(bf)


def body(n_seq, n_dp, query, key, value, grad_ctx, proj_key, proj_value):
    _, n_pos, hd = query.shape
    kp_rows = proj_key.shape[0]
    n_chunks = hd // HEAD_DIM
    n_out = n_seq // INNER
    half = kp_rows // INNER
    blk = half // n_out
    t_rows = kp_rows // n_dp
    w = HEAD_DIM
    f32, bf = jnp.float32, jnp.bfloat16
    dma = pltpu.SemaphoreType.DMA
    vmem = pl.BlockSpec(memory_space=pltpu.VMEM)
    wide = jax.ShapeDtypeStruct((n_pos, hd), bf)
    tall = jax.ShapeDtypeStruct((t_rows, n_pos), bf)
    out = pl.pallas_call(
        functools.partial(kernel, n_seq, n_dp),
        out_shape=(wide, wide, wide, tall, tall),
        in_specs=[vmem] * 6,
        out_specs=(vmem,) * 5,
        scratch_shapes=[
            pltpu.VMEM((SLOTS, half, w), f32),
            pltpu.VMEM((SLOTS, half, w), f32),
            pltpu.VMEM((SLOTS, half, w), f32),
            pltpu.VMEM((SLOTS, half, w), bf),
            pltpu.VMEM((SLOTS, half, w), bf),
            pltpu.VMEM((n_chunks, half, w), f32),
            pltpu.VMEM((n_chunks, half, w), bf),
            pltpu.VMEM((n_chunks, n_out - 1, blk, w), f32),
            pltpu.VMEM((n_chunks, n_out - 1, blk, w), bf),
            pltpu.VMEM((n_chunks, 2, kp_rows, w), bf),
            pltpu.VMEM((SLOTS, 2, half, w), f32),
            pltpu.VMEM((SLOTS, 2, half, w), bf),
            pltpu.VMEM((SLOTS, 2, half, w), bf),
            pltpu.VMEM((n_chunks, 2, half, w), bf),
            pltpu.VMEM((n_chunks, n_out - 1, 2, blk, w), bf),
            pltpu.VMEM((n_chunks, 2, kp_rows, w), bf),
            pltpu.VMEM((2, kp_rows, n_pos), f32),
            pltpu.VMEM((2, kp_rows, n_pos), bf),
            pltpu.VMEM((n_dp - 1, 2, t_rows, n_pos), bf),
            pltpu.VMEM((n_pos, kp_rows), bf),
            pltpu.VMEM((n_pos, kp_rows), bf),
            dma((5, SLOTS)),
            dma((5, RECV)),
            dma((5, n_out - 1, SLOTS)),
            dma((5, n_out - 1, RECV)),
            dma((n_dp - 1,)),
            dma((n_dp - 1,)),
        ],
        compiler_params=pltpu.CompilerParams(
            collective_id=0, has_side_effects=True, vmem_limit_bytes=56 * 2**20
        ),
    )(
        query[0], key[0], value[0], grad_ctx[0],
        proj_key, proj_value,
    )
    gq, gk, gv, sk, sv = out
    return gq[None], gk[None], gv[None], sk, sv


def solution(mesh):
    return jax.shard_map(
        functools.partial(body, mesh.shape["seq"], mesh.shape["dp"]),
        mesh=mesh,
        in_specs=(
            P("dp", "seq", None),
            P("dp", "seq", None),
            P("dp", "seq", None),
            P("dp", "seq", None),
            P(None, "seq"),
            P(None, "seq"),
        ),
        out_specs=(
            P("dp", "seq", None),
            P("dp", "seq", None),
            P("dp", "seq", None),
            P("dp", "seq"),
            P("dp", "seq"),
        ),
        check_vma=False,
    )
```

profile of v0, /device:TPU:0, one launch (start us, length us, event | category | flops | bytes accessed | tf_op | source)
XLA Modules:
  0.0 248.8 jit_solution(14071467820749372382)
XLA Ops:
  0.6 239.8 %shard_map.101 = (bf16[512,2048]{1,0:T(8,128)(2,1)}, bf16[512,2048]{1,0:T(8,128)(2,1)}, bf16[512,2048]{1,0:T(8,128)(2,1)}, bf16[128,512]{1,0:T(8,128)(2,1)}, bf16[128,512]{1,0:T(8,128)(2,1)}) custom-call(bf16[512,2048]{1,0:T(8,128)(2,1)} %bitcast.10, bf16[512,2048]{1,0:T(8,128)(2,1)} %bitcast.11, bf16[512,2048]{1,0:T(8,128)(2,1)} %bitcast.12, ...), custom_call_target="tpu_custom_call" | custom-call | tf_op jit(solution)/shard_map/pallas_call | solution.py:279
  240.5 0.0 copy-start.1
  240.5 3.3 %copy.16 = bf16[1,512,2048]{2,1,0:T(8,128)(2,1)} copy(bf16[1,512,2048]{2,1,0:T(8,128)(2,1)} %bitcast.9) | data formatting | bytes 4194304
  243.8 0.0 copy-done.1
  243.8 0.0 copy-start
  243.8 1.3 copy.17
  245.1 1.0 copy-done
  246.1 0.0 copy-start.3
  246.1 0.0 copy-start.2
  246.1 1.3 copy.18
  247.5 0.0 copy-done.3
  247.5 0.7 copy.19
  248.1 0.0 copy-done.2
  248.1 0.7 copy.20
Async XLA Ops:
  240.5 3.3 %copy-start.1 = (bf16[512,2048]{1,0:T(8,128)(2,1)S(1)}, bf16[512,2048]{1,0:T(8,128)(2,1)}, u32[]{:S(2)}) copy-start(bf16[512,2048]{1,0:T(8,128)(2,1)} %get-tuple-element.11) | copy-start | bytes 6291460
  243.8 2.3 copy-start
  246.1 1.3 copy-start.3
  246.1 2.0 copy-start.2
where the time goes:
time: 250 us; the launch traced here: 249 us
  Pallas kernels  240 us (96%)
  local copies, waits for them, and re-layouts  8.3 us (3%)
    pallas_call x1, Pallas kernels, body(): pl.pallas_call(functools.partial(kernel, n_seq, n_dp), out_shape=(wide, w...  240 us
    unnamed x13, local copies, waits for them, and re-layouts  8.3 us

commit v1 on v0

v1 whole, which is shorter than its diff:
```python
import functools

import jax
import jax.numpy as jnp
from jax import lax
from jax.experimental import pallas as pl
from jax.experimental.pallas import tpu as pltpu
from jax.sharding import PartitionSpec as P

HEAD_DIM = 128
ROOM = 2
NT = (((1,), (1,)), ((), ()))


def dot(a, b):
    return jnp.dot(a, b, preferred_element_type=jnp.float32)


def dot_nt(a, b):
    return lax.dot_general(a, b, NT, preferred_element_type=jnp.float32)


def n_bits(n_seq):
    return n_seq.bit_length() - 1


def n_slots(n_seq):
    return ROOM * n_bits(n_seq) + 2


def kernel(
    n_seq, n_dp,
    q_ref, k_ref, v_ref, g_ref, pk_ref, pv_ref,
    gq_ref, gk_ref, gv_ref, sk_ref, sv_ref,
    acc_k, acc_v, snd_v, arr_k, arr_v, full,
    acc_d, snd_d, arr_d, full_d,
    term, snd_t, arr_t, pkt_ref, pvt_ref,
    s_sem, r_sem, s_dp, r_dp,
):
    kp_rows = pk_ref.shape[0]
    n_chunks = q_ref.shape[1] // HEAD_DIM
    nb = n_bits(n_seq)
    slots = n_slots(n_seq)
    t_rows = kp_rows // n_dp
    scale = HEAD_DIM ** (-0.5)
    bf = jnp.bfloat16

    seq = lax.axis_index("seq")
    dp = lax.axis_index("dp")
    bits = [lax.rem(seq // (1 << b), 2) for b in range(nb)]
    mates = [seq + (1 - 2 * bits[b]) * (1 << b) for b in range(nb)]

    barrier = pltpu.get_barrier_semaphore()
    for b in range(nb):
        pl.semaphore_signal(barrier, inc=1, device_id={"seq": mates[b]})
    for j in range(1, n_dp):
        pl.semaphore_signal(barrier, inc=1, device_id={"dp": lax.rem(dp + j, n_dp)})
    pl.semaphore_wait(barrier, nb + n_dp - 1)

    def cols(c):
        return pl.ds(pl.multiple_of(c * HEAD_DIM, HEAD_DIM), HEAD_DIM)

    def route(c):
        t = lax.rem(c, 4) // 3
        pick = lambda a, l: [a[0] + t * (a[1] - a[0]), a[1] + t * (a[0] - a[1])] + l
        return pick(bits, bits[2:]), pick(mates, mates[2:])

    def size(s):
        return kp_rows >> (s + 1)

    def rows_at(off, s):
        return pl.ds(pl.multiple_of(off, size(s)), size(s))

    def keep(c, s):
        bit, _ = route(c)
        return rows_at(sum(bit[i] * size(i) for i in range(s + 1)), s)

    def give(c, s):
        bit, _ = route(c)
        return rows_at(sum(bit[i] * size(i) for i in range(s)) + (1 - bit[s]) * size(s), s)

    def landing(s):
        return pl.ds(kp_rows - (kp_rows >> s), size(s))

    def copy(kind, s, c, src, dst):
        slot = lax.rem(c, slots)
        return pltpu.make_async_remote_copy(
            src_ref=src, dst_ref=dst,
            send_sem=s_sem.at[kind, s, slot],
            recv_sem=r_sem.at[kind, s, slot],
            device_id={"seq": route(c)[1][s]},
        )

    def kv_copies(c, s):
        slot = lax.rem(c, slots)
        return [
            copy(0, s, c, acc_k.at[slot, give(c, s)], arr_k.at[c, landing(s)]),
            copy(1, s, c, snd_v.at[slot, give(c, s)], arr_v.at[c, landing(s)]),
        ]

    def d_copies(c, s):
        slot = lax.rem(c, slots)
        return [copy(3, s, c, snd_d.at[slot, :, give(c, s)], arr_d.at[c, :, landing(s)])]

    def gather_copies(kind, buf, c, s):
        ref = buf.at[c, :, keep(c, s)]
        return [copy(kind, s, c, ref, ref)]

    def start(copies):
        for one in copies:
            one.start()

    def wait(copies):
        for one in copies:
            one.wait()

    def send_kv(c, s):
        slot = lax.rem(c, slots)
        snd_v[slot, give(c, s)] = acc_v[slot, give(c, s)].astype(bf)
        start(kv_copies(c, s))

    def send_d(c, s):
        slot = lax.rem(c, slots)
        snd_d[slot, :, give(c, s)] = acc_d[slot, :, give(c, s)].astype(bf)
        start(d_copies(c, s))

    def stage_a(c):
        slot = lax.rem(c, slots)
        acc_k[slot] = dot(pk_ref[...], k_ref[:, cols(c)])
        acc_v[slot] = dot(pv_ref[...], v_ref[:, cols(c)])
        send_kv(c, 0)

    def sum_kv(s, c):
        slot = lax.rem(c, slots)
        wait(kv_copies(c, s))
        rows = keep(c, s)
        kt = acc_k[slot, rows] + arr_k[c, landing(s)]
        vt = acc_v[slot, rows] + arr_v[c, landing(s)].astype(jnp.float32)
        if s < nb - 1:
            acc_k[slot, rows] = kt
            acc_v[slot, rows] = vt
            send_kv(c, s + 1)
        else:
            full[c, 0, rows] = kt.astype(bf)
            full[c, 1, rows] = vt.astype(bf)
            start(gather_copies(2, full, c, s))

    def sum_d(s, c):
        slot = lax.rem(c, slots)
        wait(d_copies(c, s))
        rows = keep(c, s)
        total = acc_d[slot, :, rows] + arr_d[c, :, landing(s)].astype(jnp.float32)
        if s < nb - 1:
            acc_d[slot, :, rows] = total
            send_d(c, s + 1)
        else:
            full_d[c, :, rows] = total.astype(bf)
            start(gather_copies(4, full_d, c, s))

    def gather(kind, buf, s, c):
        wait(gather_copies(kind, buf, c, s))
        start(gather_copies(kind, buf, c, s - 1))

    def stage_e(c):
        slot = lax.rem(c, slots)
        wait(gather_copies(2, full, c, 0))
        kp = full[c, 0]
        vp = full[c, 1]
        kpt = kp.astype(jnp.float32).T.astype(bf)
        n_pos = q_ref.shape[0]
        step = min(256, n_pos)
        dk = jnp.zeros((kp_rows, HEAD_DIM), jnp.float32)
        dv = jnp.zeros((kp_rows, HEAD_DIM), jnp.float32)
        for p in range(0, n_pos, step):
            qb = q_ref[pl.ds(p, step), cols(c)]
            gb = g_ref[pl.ds(p, step), cols(c)]
            scores = dot_nt(kp, qb) * scale
            e = jnp.exp(scores - jnp.max(scores, axis=0, keepdims=True))
            probs = e * (1.0 / jnp.sum(e, axis=0, keepdims=True))
            dv += dot(probs.astype(bf), gb)
            gp = dot_nt(vp, gb)
            delta = jnp.sum(probs * gp, axis=0, keepdims=True)
            gs = (probs * (gp - delta) * scale).astype(bf)
            dk += dot(gs, qb)
            gq_ref[pl.ds(p, step), cols(c)] = dot(kpt, gs).T.astype(bf)
        acc_d[slot, 0] = dk
        acc_d[slot, 1] = dv
        send_d(c, 0)

    def stage_i(c):
        wait(gather_copies(4, full_d, c, 0))
        dkp = full_d[c, 0]
        dvp = full_d[c, 1]
        gk_ref[:, cols(c)] = dot(pkt_ref[...], dkp).astype(bf)
        gv_ref[:, cols(c)] = dot(pvt_ref[...], dvp).astype(bf)
        term[0] += dot_nt(dkp, k_ref[:, cols(c)])
        term[1] += dot_nt(dvp, v_ref[:, cols(c)])

    term[...] = jnp.zeros_like(term)

    def turn():
        pkt_ref[...] = pk_ref[...].astype(jnp.float32).T.astype(bf)
        pvt_ref[...] = pv_ref[...].astype(jnp.float32).T.astype(bf)

    stages = [stage_a]
    stages += [functools.partial(sum_kv, s) for s in range(nb)]
    stages += [functools.partial(gather, 2, full, s) for s in range(nb - 1, 0, -1)]
    stages += [stage_e]
    stages += [functools.partial(sum_d, s) for s in range(nb)]
    stages += [functools.partial(gather, 4, full_d, s) for s in range(nb - 1, 0, -1)]
    stages += [stage_i]
    heavy = (stage_e, stage_i)
    placed = list(enumerate(stages))
    order = [p for p in reversed(placed) if p[1] not in heavy] + [p for p in placed if p[1] in heavy]

    def iteration(i, _):
        pl.when(i == 1)(turn)
        for n, stage in order:
            at = n * ROOM
            pl.when((i >= at) & (i < at + n_chunks))(functools.partial(stage, i - at))
        return 0

    lax.fori_loop(0, n_chunks + ROOM * (len(stages) - 1), iteration, 0)

    snd_t[...] = term[...].astype(bf)
    copies = []
    for j in range(1, n_dp):
        to = lax.rem(dp + j, n_dp)
        rows = pl.ds(pl.multiple_of(to * t_rows, t_rows), t_rows)
        copies.append(
            pltpu.make_async_remote_copy(
                src_ref=snd_t.at[:, rows], dst_ref=arr_t.at[j - 1],
                send_sem=s_dp.at[j - 1], recv_sem=r_dp.at[j - 1],
                device_id={"dp": to},
            )
        )
    start(copies)
    wait(copies)
    total = term[:, pl.ds(pl.multiple_of(dp * t_rows, t_rows), t_rows)]
    for j in range(1, n_dp):
        total += arr_t[j - 1].astype(jnp.float32)
    sk_ref[...] = total[0].astype(bf)
    sv_ref[...] = total[1].astype(bf)


def body(n_seq, n_dp, query, key, value, grad_ctx, proj_key, proj_value):
    _, n_pos, hd = query.shape
    kp_rows = proj_key.shape[0]
    n_chunks = hd // HEAD_DIM
    nb = n_bits(n_seq)
    slots = n_slots(n_seq)
    t_rows = kp_rows // n_dp
    w = HEAD_DIM
    f32, bf = jnp.float32, jnp.bfloat16
    dma = pltpu.SemaphoreType.DMA
    vmem = pl.BlockSpec(memory_space=pltpu.VMEM)
    wide = jax.ShapeDtypeStruct((n_pos, hd), bf)
    tall = jax.ShapeDtypeStruct((t_rows, n_pos), bf)
    out = pl.pallas_call(
        functools.partial(kernel, n_seq, n_dp),
        out_shape=(wide, wide, wide, tall, tall),
        in_specs=[vmem] * 6,
        out_specs=(vmem,) * 5,
        scratch_shapes=[
            pltpu.VMEM((slots, kp_rows, w), f32),
            pltpu.VMEM((slots, kp_rows, w), f32),
            pltpu.VMEM((slots, kp_rows, w), bf),
            pltpu.VMEM((n_chunks, kp_rows, w), f32),
            pltpu.VMEM((n_chunks, kp_rows, w), bf),
            pltpu.VMEM((n_chunks, 2, kp_rows, w), bf),
            pltpu.VMEM((slots, 2, kp_rows, w), f32),
            pltpu.VMEM((slots, 2, kp_rows, w), bf),
            pltpu.VMEM((n_chunks, 2, kp_rows, w), bf),
            pltpu.VMEM((n_chunks, 2, kp_rows, w), bf),
            pltpu.VMEM((2, kp_rows, n_pos), f32),
            pltpu.VMEM((2, kp_rows, n_pos), bf),
            pltpu.VMEM((n_dp - 1, 2, t_rows, n_pos), bf),
            pltpu.VMEM((n_pos, kp_rows), bf),
            pltpu.VMEM((n_pos, kp_rows), bf),
            dma((5, nb, slots)),
            dma((5, nb, slots)),
            dma((n_dp - 1,)),
            dma((n_dp - 1,)),
        ],
        compiler_params=pltpu.CompilerParams(
            collective_id=0, has_side_effects=True, vmem_limit_bytes=60 * 2**20
        ),
    )(
        query[0], key[0], value[0], grad_ctx[0],
        proj_key, proj_value,
    )
    gq, gk, gv, sk, sv = out
    return gq[None], gk[None], gv[None], sk, sv


def solution(mesh):
    return jax.shard_map(
        functools.partial(body, mesh.shape["seq"], mesh.shape["dp"]),
        mesh=mesh,
        in_specs=(
            P("dp", "seq", None),
            P("dp", "seq", None),
            P("dp", "seq", None),
            P("dp", "seq", None),
            P(None, "seq"),
            P(None, "seq"),
        ),
        out_specs=(
            P("dp", "seq", None),
            P("dp", "seq", None),
            P("dp", "seq", None),
            P("dp", "seq"),
            P("dp", "seq"),
        ),
        check_vma=False,
    )
```

time: 250 us -> 229 us (0.916)
  Pallas kernels: 240 us -> 220 us
    pallas_call x1, Pallas kernels: 240 us -> 220 us  [body(): pl.pallas_call(functools.partial(kernel, n_seq, n_dp), out_shape=(wide, w...]
where the time goes in v1:
time: 229 us; the launch traced here: 228 us
  Pallas kernels  220 us (96%)
  local copies, waits for them, and re-layouts  8.3 us (4%)
    pallas_call x1, Pallas kernels, body(): pl.pallas_call(functools.partial(kernel, n_seq, n_dp), out_shape=(wide, w...  220 us
    unnamed x13, local copies, waits for them, and re-layouts  8.3 us

profile of v1, /device:TPU:0, one launch (start us, length us, event | category | flops | bytes accessed | tf_op | source)
XLA Modules:
  0.0 228.5 jit_solution(14217264171811681392)
XLA Ops:
  0.6 219.5 %shard_map.101 = (bf16[512,2048]{1,0:T(8,128)(2,1)}, bf16[512,2048]{1,0:T(8,128)(2,1)}, bf16[512,2048]{1,0:T(8,128)(2,1)}, bf16[128,512]{1,0:T(8,128)(2,1)}, bf16[128,512]{1,0:T(8,128)(2,1)}) custom-call(bf16[512,2048]{1,0:T(8,128)(2,1)} %bitcast.10, bf16[512,2048]{1,0:T(8,128)(2,1)} %bitcast.11, bf16[512,2048]{1,0:T(8,128)(2,1)} %bitcast.12, ...), custom_call_target="tpu_custom_call" | custom-call | tf_op jit(solution)/shard_map/pallas_call | solution.py:259
  220.2 0.0 copy-start.1
  220.2 3.3 %copy.16 = bf16[1,512,2048]{2,1,0:T(8,128)(2,1)} copy(bf16[1,512,2048]{2,1,0:T(8,128)(2,1)} %bitcast.9) | data formatting | bytes 4194304
  223.5 0.0 copy-done.1
  223.5 0.0 copy-start
  223.5 1.3 copy.17
  224.8 1.0 copy-done
  225.8 0.0 copy-start.3
  225.8 0.0 copy-start.2
  225.8 1.3 copy.18
  227.1 0.0 copy-done.3
  227.1 0.7 copy.19
  227.8 0.0 copy-done.2
  227.8 0.7 copy.20
Async XLA Ops:
  220.2 3.3 %copy-start.1 = (bf16[512,2048]{1,0:T(8,128)(2,1)S(1)}, bf16[512,2048]{1,0:T(8,128)(2,1)}, u32[]{:S(2)}) copy-start(bf16[512,2048]{1,0:T(8,128)(2,1)} %get-tuple-element.11) | copy-start | bytes 6291460
  223.5 2.3 %copy-start = (bf16[512,2048]{1,0:T(8,128)(2,1)S(1)}, bf16[512,2048]{1,0:T(8,128)(2,1)}, u32[]{:S(2)}) copy-start(bf16[512,2048]{1,0:T(8,128)(2,1)} %get-tuple-element.12) | copy-start | bytes 6291460
  225.8 1.3 copy-start.3
  225.8 2.0 copy-start.2

commit v2 on v1

--- a/solution.py
+++ b/solution.py
@@ -8,7 +8,7 @@
 from jax.sharding import PartitionSpec as P
 
 HEAD_DIM = 128
-ROOM = 2
+ROOM = 1
 NT = (((1,), (1,)), ((), ()))
 
 
@@ -25,7 +25,7 @@
 
 
 def n_slots(n_seq):
-    return ROOM * n_bits(n_seq) + 2
+    return ROOM * n_bits(n_seq) + 5
 
 
 def kernel(
@@ -209,13 +209,9 @@
     stages += [functools.partial(sum_d, s) for s in range(nb)]
     stages += [functools.partial(gather, 4, full_d, s) for s in range(nb - 1, 0, -1)]
     stages += [stage_i]
-    heavy = (stage_e, stage_i)
-    placed = list(enumerate(stages))
-    order = [p for p in reversed(placed) if p[1] not in heavy] + [p for p in placed if p[1] in heavy]
-
     def iteration(i, _):
         pl.when(i == 1)(turn)
-        for n, stage in order:
+        for n, stage in enumerate(stages):
             at = n * ROOM
             pl.when((i >= at) & (i < at + n_chunks))(functools.partial(stage, i - at))
         return 0

time: 229 us -> 229 us (level)
  Pallas kernels: 220 us -> 217 us
where the time goes in v2:
time: 229 us; the launch traced here: 226 us
  Pallas kernels  217 us (95%)
  local copies, waits for them, and re-layouts  8.3 us (4%)
    pallas_call x1, Pallas kernels, body(): pl.pallas_call(functools.partial(kernel, n_seq, n_dp), out_shape=(wide, w...  217 us
    unnamed x13, local copies, waits for them, and re-layouts  8.3 us

profile of v2, /device:TPU:0, one launch (start us, length us, event | category | flops | bytes accessed | tf_op | source)
XLA Modules:
  0.0 226.3 jit_solution(243745767591487127)
XLA Ops:
  0.6 217.3 %shard_map.101 = (bf16[512,2048]{1,0:T(8,128)(2,1)}, bf16[512,2048]{1,0:T(8,128)(2,1)}, bf16[512,2048]{1,0:T(8,128)(2,1)}, bf16[128,512]{1,0:T(8,128)(2,1)}, bf16[128,512]{1,0:T(8,128)(2,1)}) custom-call(bf16[512,2048]{1,0:T(8,128)(2,1)} %bitcast.10, bf16[512,2048]{1,0:T(8,128)(2,1)} %bitcast.11, bf16[512,2048]{1,0:T(8,128)(2,1)} %bitcast.12, ...), custom_call_target="tpu_custom_call" | custom-call | tf_op jit(solution)/shard_map/pallas_call | solution.py:255
  217.9 0.0 copy-start.1
  218.0 3.3 %copy.16 = bf16[1,512,2048]{2,1,0:T(8,128)(2,1)} copy(bf16[1,512,2048]{2,1,0:T(8,128)(2,1)} %bitcast.9) | data formatting | bytes 4194304
  221.3 0.0 copy-done.1
  221.3 0.0 copy-start
  221.3 1.3 copy.17
  222.6 1.0 copy-done
  223.6 0.0 copy-start.3
  223.6 0.0 copy-start.2
  223.6 1.3 copy.18
  224.9 0.0 copy-done.3
  224.9 0.7 copy.19
  225.6 0.0 copy-done.2
  225.6 0.7 copy.20
Async XLA Ops:
  217.9 3.3 %copy-start.1 = (bf16[512,2048]{1,0:T(8,128)(2,1)S(1)}, bf16[512,2048]{1,0:T(8,128)(2,1)}, u32[]{:S(2)}) copy-start(bf16[512,2048]{1,0:T(8,128)(2,1)} %get-tuple-element.11) | copy-start | bytes 6291460
  221.3 2.3 %copy-start = (bf16[512,2048]{1,0:T(8,128)(2,1)S(1)}, bf16[512,2048]{1,0:T(8,128)(2,1)}, u32[]{:S(2)}) copy-start(bf16[512,2048]{1,0:T(8,128)(2,1)} %get-tuple-element.12) | copy-start | bytes 6291460
  223.6 1.3 copy-start.3
  223.6 2.0 copy-start.2

commit v3 on v2

--- a/solution.py
+++ b/solution.py
@@ -8,7 +8,6 @@
 from jax.sharding import PartitionSpec as P
 
 HEAD_DIM = 128
-ROOM = 1
 NT = (((1,), (1,)), ((), ()))
 
 
@@ -25,7 +24,7 @@
 
 
 def n_slots(n_seq):
-    return ROOM * n_bits(n_seq) + 5
+    return n_bits(n_seq) + 5
 
 
 def kernel(
@@ -209,14 +208,20 @@
     stages += [functools.partial(sum_d, s) for s in range(nb)]
     stages += [functools.partial(gather, 4, full_d, s) for s in range(nb - 1, 0, -1)]
     stages += [stage_i]
+    starts, at = [], 0
+    for n in range(len(stages)):
+        if n in (1, 2 * nb, 2 * nb + 1, 4 * nb):
+            at += 1
+        at += n > 0
+        starts.append(at)
+
     def iteration(i, _):
         pl.when(i == 1)(turn)
-        for n, stage in enumerate(stages):
-            at = n * ROOM
+        for at, stage in zip(starts, stages):
             pl.when((i >= at) & (i < at + n_chunks))(functools.partial(stage, i - at))
         return 0
 
-    lax.fori_loop(0, n_chunks + ROOM * (len(stages) - 1), iteration, 0)
+    lax.fori_loop(0, n_chunks + starts[-1], iteration, 0)
 
     snd_t[...] = term[...].astype(bf)
     copies = []

time: 229 us -> 230 us (level)
  Pallas kernels: 217 us -> 220 us
    pallas_call x1, Pallas kernels: 217 us -> 220 us  [body(): pl.pallas_call(functools.partial(kernel, n_seq, n_dp), out_shape=(wide, w...]
where the time goes in v3:
time: 230 us; the launch traced here: 229 us
  Pallas kernels  220 us (96%)
  local copies, waits for them, and re-layouts  8.3 us (4%)
    pallas_call x1, Pallas kernels, body(): pl.pallas_call(functools.partial(kernel, n_seq, n_dp), out_shape=(wide, w...  220 us
    unnamed x13, local copies, waits for them, and re-layouts  8.3 us

profile of v3, /device:TPU:0, one launch (start us, length us, event | category | flops | bytes accessed | tf_op | source)
XLA Modules:
  0.0 229.4 jit_solution(3805476096320144899)
XLA Ops:
  0.6 220.5 %shard_map.101 = (bf16[512,2048]{1,0:T(8,128)(2,1)}, bf16[512,2048]{1,0:T(8,128)(2,1)}, bf16[512,2048]{1,0:T(8,128)(2,1)}, bf16[128,512]{1,0:T(8,128)(2,1)}, bf16[128,512]{1,0:T(8,128)(2,1)}) custom-call(bf16[512,2048]{1,0:T(8,128)(2,1)} %bitcast.10, bf16[512,2048]{1,0:T(8,128)(2,1)} %bitcast.11, bf16[512,2048]{1,0:T(8,128)(2,1)} %bitcast.12, ...), custom_call_target="tpu_custom_call" | custom-call | tf_op jit(solution)/shard_map/pallas_call | solution.py:260
  221.1 0.0 copy-start.1
  221.1 3.3 %copy.16 = bf16[1,512,2048]{2,1,0:T(8,128)(2,1)} copy(bf16[1,512,2048]{2,1,0:T(8,128)(2,1)} %bitcast.9) | data formatting | bytes 4194304
  224.4 0.0 copy-done.1
  224.4 0.0 copy-start
  224.4 1.3 copy.17
  225.7 1.0 copy-done
  226.8 0.0 copy-start.3
  226.8 0.0 copy-start.2
  226.8 1.3 copy.18
  228.1 0.0 copy-done.3
  228.1 0.7 copy.19
  228.8 0.0 copy-done.2
  228.8 0.7 copy.20
Async XLA Ops:
  221.1 3.3 %copy-start.1 = (bf16[512,2048]{1,0:T(8,128)(2,1)S(1)}, bf16[512,2048]{1,0:T(8,128)(2,1)}, u32[]{:S(2)}) copy-start(bf16[512,2048]{1,0:T(8,128)(2,1)} %get-tuple-element.11) | copy-start | bytes 6291460
  224.4 2.3 %copy-start = (bf16[512,2048]{1,0:T(8,128)(2,1)S(1)}, bf16[512,2048]{1,0:T(8,128)(2,1)}, u32[]{:S(2)}) copy-start(bf16[512,2048]{1,0:T(8,128)(2,1)} %get-tuple-element.12) | copy-start | bytes 6291460
  226.8 1.3 copy-start.3
  226.8 2.0 copy-start.2
